TPU v7x, 256 devices: a whole 4x4x8 slice. The times are simulated.
256 devices in a mesh: dp: 32 (over z, x), eig: 2 (over y_lo), tensor: 4 (over y_hi, core).
Axes of the slice: x: 4, y: 4 (y_hi: 2, y_lo: 2; y = y_hi * 2 + y_lo), z: 8, core: 2. Of those that a mesh axis runs over, the one named last changes fastest.
Arguments:
- rotary_queries: bfloat16 [32, 2048, 4096], P('dp', None, ('eig', 'tensor')), may hold values from -180 to 180
- rotary_keys: bfloat16 [32, 2048, 4096], P('dp', None, ('eig', 'tensor')), may hold values from -6 to 6
- value_matrix: bfloat16 [32, 2048, 4096], P('dp', None, ('eig', 'tensor')), may hold values from -6 to 6
- document_index: int32 [32, 2048], P('dp'), may hold values from 0 to 7, never falling along the last dimension, each value on 1 to 1024 neighbouring positions
- cotangent: bfloat16 [32, 2048, 8192], P('dp', None, ('eig', 'tensor')), may hold values from -6 to 6
- adapter_up_weight: bfloat16 [8192, 16], P(('eig', 'tensor')), may hold values from -0.5 to 0.5
- input_eigenvectors: bfloat16 [4096, 4096], P(('eig', 'tensor'), 'dp'), may hold values from -0.09375 to 0.09375
Outputs:
- spectrum: float32 [16, 4096], P(('eig', 'tensor'), 'dp')
Inputs may be any that keep to these rules, and one draw needn't show every extreme that they name: `document_index`: document ids never fall along a sequence; each document has 1 to 1024 positions.
All inputs are finite; a program needn't handle non-finite values.
Results may differ from a plain program's by a relative error of at most 0.003.
Values may be sent and summed in bfloat16 or wider, within the bound.
A program may use at most 128 MiB of HBM per device.

v0:
```python
import jax
import jax.numpy as jnp
from jax import lax
from jax.sharding import PartitionSpec as P

HEAD_DIM = 128
LEN = 2048


def shards(
    rotary_queries,
    rotary_keys,
    value_matrix,
    document_index,
    cotangent,
    adapter_up_weight,
    input_eigenvectors,
):
    heads_here = rotary_queries.shape[2] // HEAD_DIM
    lower_portion = jnp.dot(cotangent[0], adapter_up_weight, preferred_element_type=jnp.float32)
    reduced_rank = lax.psum(lower_portion, ("eig", "tensor")).astype(jnp.bfloat16)
    split_q = rotary_queries[0].reshape(LEN, heads_here, HEAD_DIM)
    split_k = rotary_keys[0].reshape(LEN, heads_here, HEAD_DIM)
    split_v = value_matrix[0].reshape(LEN, heads_here, HEAD_DIM)
    document = document_index[0]
    position = jnp.arange(LEN, dtype=jnp.int32)
    block = min(512, LEN)

    def attend_block(block_index):
        start = block_index * block
        query_block = lax.dynamic_slice_in_dim(split_q, start, block, 0)
        query_doc = lax.dynamic_slice_in_dim(document, start, block, 0)
        query_pos = start + jnp.arange(block, dtype=jnp.int32)
        scores = jnp.einsum(
            "qhd,khd->hqk", query_block, split_k, preferred_element_type=jnp.float32
        ) * HEAD_DIM ** (-0.5)
        allowed = (query_doc[:, None] == document[None, :]) & (
            position[None, :] <= query_pos[:, None]
        )
        scores = jnp.where(allowed[None], scores, -1e30)
        row_max = jnp.max(scores, axis=-1, keepdims=True)
        expon = jnp.exp(scores - row_max)
        row_total = jnp.sum(expon, axis=-1, keepdims=True)
        weights = (expon / row_total).astype(jnp.bfloat16)
        result = jnp.einsum(
            "hqk,khd->qhd", weights, split_v, preferred_element_type=jnp.float32
        ).astype(jnp.bfloat16)
        return result.reshape(block, heads_here * HEAD_DIM)

    mixed = lax.map(attend_block, jnp.arange(LEN // block, dtype=jnp.int32)).reshape(
        LEN, heads_here * HEAD_DIM
    )
    grad_full = lax.dot_general(
        reduced_rank, mixed, (((0,), (0,)), ((), ())), preferred_element_type=jnp.float32
    )
    grad = (grad_full * LEN ** (-0.5)).astype(jnp.bfloat16)
    rotated = jnp.dot(
        grad,
        lax.all_gather(input_eigenvectors, "dp", axis=1, tiled=True),
        preferred_element_type=jnp.float32,
    )
    own_rows = lax.psum_scatter(rotated, ("eig", "tensor"), scatter_dimension=0, tiled=True)
    spectrum = lax.psum_scatter(
        own_rows * own_rows, "dp", scatter_dimension=1, tiled=True
    ) / lax.axis_size("dp")
    return spectrum


def solution(mesh):
    return jax.shard_map(
        shards,
        mesh=mesh,
        in_specs=(
            P("dp", None, ("eig", "tensor")),
            P("dp", None, ("eig", "tensor")),
            P("dp", None, ("eig", "tensor")),
            P("dp", None),
            P("dp", None, ("eig", "tensor")),
            P(("eig", "tensor"), None),
            P(("eig", "tensor"), "dp"),
        ),
        out_specs=P(("eig", "tensor"), "dp"),
        check_vma=False,
    )
```

profile of v0, /device:TPU:1, one launch (start us, length us, event | category | flops | bytes accessed | tf_op | source)
XLA Modules:
  0.0 440.5 jit_solution(4945027726512707814)
XLA Ops:
  6.5 0.7 all-gather.2.cloned.1.call-update
  7.3 0.0 all-reduce.4.cloned.1.call-start
  7.3 2.9 copy.16
  10.3 2.5 copy.19
  12.8 4.0 copy.15
  16.7 4.1 copy.17
  20.8 3.4 fusion.25
  24.2 27.7 %all-reduce.5 = bf16[2048,16]{0,1:T(8,128)(2,1)S(1)} all-reduce(f32[2048,16]{0,1:T(8,128)S(1)} %fusion.25), channel_id=1, replica_groups=mesh['dp'=32,'eig'=2,'tensor'=4] {'eig','tensor'}, use_global_device_ids=true, to_apply=%region_0.0 | all-reduce | flops 32768 | bytes 196608 | tf_op jit(solution)/shard_map/psum | solution.py:21
  52.0 0.0 copy-done.1
  52.0 0.0 copy-done.2
  52.0 94.1 %while.11 = (s32[]{:T(128)}, bf16[4,512,512]{2,1,0:T(8,128)(2,1)S(1)}, s32[4]{0:T(128)S(1)}, s32[2048]{0:T(1024)S(1)}, s32[1,2048]{1,0:T(1,128)S(1)}, /*index=5*...) while((s32[]{:T(128)}, ...), condition=%wide.region_4.5_spmd.clone, body=%wide.region_1.4_spmd.clone.sunk | while | flops 2176059904 | bytes 43026620 | solution.py:50
  52.0 0.6 dynamic_slice.29
  53.2 0.1 dynamic_slice.30
  53.2 1.2 fusion.54
  54.4 11.4 %fusion.55 = (f32[4,512]{1,0:T(4,128)S(1)}, f32[4,512,2048]{2,1,0:T(8,128)}) fusion(pred[512,2048]{1,0:T(8,128)(4,1)S(1)} %fusion.54, bf16[2048,4,128]{2,0,1:T(8,128)(2,1)} %get-tuple-element.188, bf16[2048,4,128]{0,2,1:T(8,128)(2,1)} %get-tuple-element.187, s32[]{:T(128)S(6)} %select_n.23), kind=kOutput, calls=%fused_computation.33.clone.1 | convolution fusion | flops 1090521088 | bytes 20455428 | tf_op jit(solution)/shard_map/while/body/eval_jaxpr/sub | solution.py:42
  65.8 9.5 %fusion.56 = bf16[4,512,128]{1,2,0:T(8,128)(2,1)S(1)} fusion(bf16[2048,4,128]{0,2,1:T(8,128)(2,1)} %get-tuple-element.189, f32[4,512,2048]{2,1,0:T(8,128)} %get-tuple-element.156, f32[4,512]{1,0:T(4,128)S(1)} %get-tuple-element.157), kind=kOutput, calls=%fused_computation.13.clone.1 | convolution fusion | flops 1082392576 | bytes 19406848 | tf_op jit(solution)/shard_map/while/body/eval_jaxpr/hqk,khd->qhd/dot_general | solution.py:45
  75.3 0.2 copy.27
  75.6 0.6 dynamic_slice.29
  76.7 0.1 dynamic_slice.30
  76.8 1.2 fusion.54
  78.0 11.4 %fusion.55 = (f32[4,512]{1,0:T(4,128)S(1)}, f32[4,512,2048]{2,1,0:T(8,128)}) fusion(pred[512,2048]{1,0:T(8,128)(4,1)S(1)} %fusion.54, bf16[2048,4,128]{2,0,1:T(8,128)(2,1)} %get-tuple-element.188, bf16[2048,4,128]{0,2,1:T(8,128)(2,1)} %get-tuple-element.187, s32[]{:T(128)S(6)} %select_n.23), kind=kOutput, calls=%fused_computation.33.clone.1 | convolution fusion | flops 1090521088 | bytes 20455428 | tf_op jit(solution)/shard_map/while/body/eval_jaxpr/sub | solution.py:42
  89.4 9.4 %fusion.56 = bf16[4,512,128]{1,2,0:T(8,128)(2,1)S(1)} fusion(bf16[2048,4,128]{0,2,1:T(8,128)(2,1)} %get-tuple-element.189, f32[4,512,2048]{2,1,0:T(8,128)} %get-tuple-element.156, f32[4,512]{1,0:T(4,128)S(1)} %get-tuple-element.157), kind=kOutput, calls=%fused_computation.13.clone.1 | convolution fusion | flops 1082392576 | bytes 19406848 | tf_op jit(solution)/shard_map/while/body/eval_jaxpr/hqk,khd->qhd/dot_general | solution.py:45
  98.9 0.2 copy.27
  99.2 0.6 dynamic_slice.29
  100.3 0.1 dynamic_slice.30
  100.4 1.2 fusion.54
  101.6 11.4 %fusion.55 = (f32[4,512]{1,0:T(4,128)S(1)}, f32[4,512,2048]{2,1,0:T(8,128)}) fusion(pred[512,2048]{1,0:T(8,128)(4,1)S(1)} %fusion.54, bf16[2048,4,128]{2,0,1:T(8,128)(2,1)} %get-tuple-element.188, bf16[2048,4,128]{0,2,1:T(8,128)(2,1)} %get-tuple-element.187, s32[]{:T(128)S(6)} %select_n.23), kind=kOutput, calls=%fused_computation.33.clone.1 | convolution fusion | flops 1090521088 | bytes 20455428 | tf_op jit(solution)/shard_map/while/body/eval_jaxpr/sub | solution.py:42
  113.0 9.4 %fusion.56 = bf16[4,512,128]{1,2,0:T(8,128)(2,1)S(1)} fusion(bf16[2048,4,128]{0,2,1:T(8,128)(2,1)} %get-tuple-element.189, f32[4,512,2048]{2,1,0:T(8,128)} %get-tuple-element.156, f32[4,512]{1,0:T(4,128)S(1)} %get-tuple-element.157), kind=kOutput, calls=%fused_computation.13.clone.1 | convolution fusion | flops 1082392576 | bytes 19406848 | tf_op jit(solution)/shard_map/while/body/eval_jaxpr/hqk,khd->qhd/dot_general | solution.py:45
  122.3 0.2 copy.27
  122.6 0.6 dynamic_slice.29
  123.8 0.1 dynamic_slice.30
  123.8 1.2 fusion.54
  125.0 11.4 %fusion.55 = (f32[4,512]{1,0:T(4,128)S(1)}, f32[4,512,2048]{2,1,0:T(8,128)}) fusion(pred[512,2048]{1,0:T(8,128)(4,1)S(1)} %fusion.54, bf16[2048,4,128]{2,0,1:T(8,128)(2,1)} %get-tuple-element.188, bf16[2048,4,128]{0,2,1:T(8,128)(2,1)} %get-tuple-element.187, s32[]{:T(128)S(6)} %select_n.23), kind=kOutput, calls=%fused_computation.33.clone.1 | convolution fusion | flops 1090521088 | bytes 20455428 | tf_op jit(solution)/shard_map/while/body/eval_jaxpr/sub | solution.py:42
  136.4 9.4 %fusion.56 = bf16[4,512,128]{1,2,0:T(8,128)(2,1)S(1)} fusion(bf16[2048,4,128]{0,2,1:T(8,128)(2,1)} %get-tuple-element.189, f32[4,512,2048]{2,1,0:T(8,128)} %get-tuple-element.156, f32[4,512]{1,0:T(4,128)S(1)} %get-tuple-element.157), kind=kOutput, calls=%fused_computation.13.clone.1 | convolution fusion | flops 1082392576 | bytes 19406848 | tf_op jit(solution)/shard_map/while/body/eval_jaxpr/hqk,khd->qhd/dot_general | solution.py:45
  145.8 0.2 copy.27
  146.1 0.0 copy-start.3
  146.1 0.0 all-gather.2.cloned.1.call-done
  146.1 3.9 fusion.28
  150.0 0.0 all-reduce.4.cloned.1.call-update
  150.0 0.0 reduce-scatter.4.cloned.1.call-start
  150.1 0.6 dynamic-slice
  151.3 64.3 %all-reduce.4.cloned.1.call-done = f32[16,4096]{1,0:T(8,128)} async-done(((f32[16,4096]{1,0:T(8,128)}), f32[16,4096]{1,0:T(8,128)}) %all-reduce.4.cloned.1.call-update) | async-done | bytes 262160
  215.6 0.9 dynamic-slice_multiply_fusion
  216.6 2.0 copy.21
  218.6 0.0 reduce-scatter.4.cloned.1.call-update
  218.6 213.9 %reduce-scatter.4.cloned.1.call-done = f32[128,2]{1,0:T(8,128)} async-done(((f32[4096,2]{1,0:T(8,128)}), f32[128,2]{1,0:T(8,128)}) %reduce-scatter.4.cloned.1.call-update) | async-done | bytes 1040
  432.4 0.9 copy.22
  433.3 0.6 broadcast_multiply_fusion
  (16 shorter events, 0.2 us)
Async XLA Ops:
  6.5 14.3 %copy-start = (bf16[1024,16]{0,1:T(8,128)(2,1)S(1)}, bf16[1024,16]{0,1:T(8,128)(2,1)}, u32[]{:S(2)}) copy-start(bf16[1024,16]{0,1:T(8,128)(2,1)} %param.14) | copy-start | bytes 98308
  6.5 139.6 %all-gather.2.cloned.1.call-start = ((), (), s32[]{:S(2)}) async-start(), calls=%async_computation.1 | async-start | bytes 4325376 | tf_op jit(solution)/shard_map/all_gather | solution.py:59
  7.3 208.4 %all-reduce.4.cloned.1.call-start = ((), (), s32[]{:S(2)}) async-start(), calls=%async_computation.3 | async-start | bytes 524288
  16.7 35.2 %copy-start.1 = (bf16[4,512,512]{2,1,0:T(8,128)(2,1)S(1)}, bf16[4,512,512]{2,1,0:T(8,128)(2,1)}, u32[]{:S(2)}) copy-start(bf16[4,512,512]{2,1,0:T(8,128)(2,1)} %custom-call) | copy-start | bytes 6291460
  16.7 35.2 %copy-start.2 = (s32[1,2048]{1,0:T(1,128)S(1)}, s32[1,2048]{1,0:T(1,128)}, u32[]{:S(2)}) copy-start(s32[1,2048]{1,0:T(1,128)} %param.12) | copy-start | bytes 24580
  146.1 4.0 copy-start.3
  150.0 282.4 %reduce-scatter.4.cloned.1.call-start = ((), (), s32[]{:S(2)}) async-start(), calls=%async_computation.2 | async-start | bytes 2162688
Sparse Core Ops, SparseCore 0:
  9.8 83.7 all-gather.1
  150.1 65.4 all-reduce.3
  220.0 212.4 reduce-scatter.3
where the time goes:
time: 445 us; the launch traced here: 440 us
  waiting for transfers between devices  279 us (63%)
  matrix products  90.5 us (20%)
  blocking collectives  27.7 us (6%)
  local copies, waits for them, and re-layouts  20.7 us (5%)
  between operations  13.8 us (3%)
  other arithmetic  6.28 us (1%)
    unnamed x5, waiting for transfers between devices  279 us
    sub x4, matrix products, attend_block(): expon = jnp.exp(scores - row_max)  45.6 us
    dot_general x4, matrix products, attend_block(): jnp.einsum('hqk,khd->qhd', weights, split_v, preferred_element_type=jnp.f...  37.6 us
    psum x1, blocking collectives, shards(): lax.psum(lower_portion, ('eig', 'tensor')).astype(jnp.bfloat16)  27.7 us
    unnamed x15, local copies, waits for them, and re-layouts  17 us
  transfers between devices with their start and end apart: 3, of which 2 were waited for; matrix products, arithmetic and copies ran while one was open for 25% of the time, Pallas kernels for 0%

commit v1 on v0

v1 whole, which is shorter than its diff:
```python
import math

import jax
import jax.numpy as jnp
from jax import lax
from jax.experimental import pallas as pl
from jax.experimental.pallas import tpu as pltpu
from jax.sharding import PartitionSpec as P

HEAD_DIM = 128
HEADS = 4
LEN = 2048
RANK = 16
COLS = HEADS * HEAD_DIM
FEATURES = 1024
SEQS = 32
WINDOW = 1024
BLOCK = 256
BLOCKS = LEN // BLOCK
SCALE = math.log2(math.e) / math.sqrt(HEAD_DIM)
HALF = LEN // 2
NEG = -1e30
MESH = pl.DeviceIdType.MESH
f32 = jnp.float32
bf16 = jnp.bfloat16


def dot(a, b, ca=1, cb=0):
    return lax.dot_general(a, b, (((ca,), (cb,)), ((), ())), preferred_element_type=f32)


def places():
    dp = lax.axis_index("dp")
    eig = lax.axis_index("eig")
    tensor = lax.axis_index("tensor")
    return dp // 4, lax.rem(dp, 4), 2 * (tensor // 2) + eig, lax.rem(tensor, 2)


def device(z, x, y, core):
    return {"dp": 4 * z + x, "eig": lax.rem(y, 2), "tensor": 2 * (y // 2) + core}


def kernel(
    q_hbm, k_hbm, v_hbm, doc_hbm, cot_hbm, up_hbm, vec_hbm, out_ref,
    q, k, v, doc, cot, up, vec, kx, qx, perm, mixed,
    low_part, low_core, low_send, low_y, low,
    grads, part, part_core, rot_send, rot_y, spec_send, spec_x,
    in_sem, cot_sem, sc_send, sc_recv, sy_send, sy_recv, sx_send, sx_recv, sz_send, sz_recv,
):
    z, x, y, core = places()
    other = device(z, x, y, 1 - core)
    y_to = [device(z, x, lax.rem(y + d, 4), core) for d in range(1, 4)]
    x_to = [device(z, lax.rem(x + d, 4), y, core) for d in range(1, 4)]
    x_from = [device(z, lax.rem(x + 4 - d, 4), y, core) for d in range(1, 4)]
    z_to = [device(lax.rem(z + d, 8), x, y, core) for d in range(1, 8)]
    peers = [other] + y_to + x_to + z_to

    def remote(src, dst, send, recv, to):
        return pltpu.make_async_remote_copy(
            src_ref=src, dst_ref=dst, send_sem=send, recv_sem=recv, device_id=to, device_id_type=MESH
        )

    barrier = pltpu.get_barrier_semaphore()
    for peer in peers:
        pl.semaphore_signal(barrier, inc=1, device_id=peer, device_id_type=MESH)

    loads = [
        pltpu.make_async_copy(src, dst, in_sem.at[n])
        for n, (src, dst) in enumerate(
            [
                (up_hbm, up),
                (doc_hbm, doc),
                (q_hbm.at[0], q),
                (k_hbm.at[0], k),
                (v_hbm.at[0], v),
                (vec_hbm, vec.at[0]),
            ]
        )
    ]
    chunks = [
        pltpu.make_async_copy(
            cot_hbm.at[0, pl.ds(512 * c, 512), :], cot.at[pl.ds(512 * c, 512), :], cot_sem.at[c]
        )
        for c in range(4)
    ]
    loads[0].start()
    loads[1].start()
    for c in chunks:
        c.start()
    for c in loads[2:]:
        c.start()

    loads[1].wait()
    one_hot = jnp.where(
        lax.broadcasted_iota(jnp.int32, (HEAD_DIM, LEN), 0) == doc[...], 1.0, 0.0
    ).astype(f32)
    turned = one_hot.T
    kx[...] = turned.astype(bf16)
    qx[...] = jnp.where(turned > 0.5, 0.0, NEG).astype(bf16)
    row = lax.broadcasted_iota(jnp.int32, (128, 128), 0)
    source = (
        16 * ((row >> 1) & 7) + 8 * ((row >> 4) & 1) + 4 * ((row >> 5) & 1) + 2 * (row >> 6) + (row & 1)
    )
    perm[...] = jnp.where(lax.broadcasted_iota(jnp.int32, (128, 128), 1) == source, 1.0, 0.0).astype(bf16)

    loads[0].wait()
    up_t = up[...].astype(f32).T.astype(bf16)
    for c in range(4):
        chunks[c].wait()
        low_part[c // 2, :, pl.ds(512 * (c % 2), 512)] = dot(
            up_t, cot[512 * c : 512 * (c + 1), :], 1, 1
        )
    for c in loads[2:]:
        c.wait()

    lower = lax.broadcasted_iota(jnp.int32, (BLOCK, BLOCK), 1) <= lax.broadcasted_iota(
        jnp.int32, (BLOCK, BLOCK), 0
    )
    ones = jnp.ones((BLOCK, HEAD_DIM), bf16)

    def scores(h, i):
        hs = slice(h * HEAD_DIM, (h + 1) * HEAD_DIM)
        rows = slice(i * BLOCK, (i + 1) * BLOCK)
        first = max(0, (i * BLOCK - WINDOW + 1) // BLOCK)
        query = jnp.concatenate([q[rows, hs], qx[rows, :]], axis=1)
        result = []
        for j in range(first, i + 1):
            at = slice(j * BLOCK, (j + 1) * BLOCK)
            key = jnp.concatenate([k[at, hs], kx[at, :]], axis=1)
            s = dot(query, key, 1, 1)
            result.append(jnp.where(lower, s, NEG) if j == i else s)
        return first, result

    def mix(h, i, first, blocks):
        hs = slice(h * HEAD_DIM, (h + 1) * HEAD_DIM)
        top = blocks[0]
        for s in blocks[1:]:
            top = jnp.maximum(top, s)
        top = jnp.max(top, axis=1, keepdims=True)
        total = None
        for n, s in enumerate(blocks):
            at = slice((first + n) * BLOCK, (first + n + 1) * BLOCK)
            weights = jnp.exp2((s - top) * SCALE).astype(bf16)
            term = dot(weights, jnp.concatenate([v[at, hs], ones], axis=1))
            total = term if total is None else total + term
        mixed[i * BLOCK : (i + 1) * BLOCK, hs] = (
            total[:, :HEAD_DIM] / total[:, HEAD_DIM:]
        ).astype(bf16)

    sent = []

    def send_low_core():
        pl.semaphore_wait(barrier, len(peers))
        c = remote(low_part.at[1 - core], low_core, sc_send.at[0], sc_recv.at[0], other)
        c.start()
        sent.append(c)
        for d in range(1, 4):
            e = remote(vec.at[0], vec.at[d], sx_send.at[d - 1], sx_recv.at[d - 1], x_to[d - 1])
            e.start()
            sent.append(e)

    def send_low_y():
        sent[0].wait_recv()
        mine = low_part[core] + low_core[...]
        low_part[core] = mine
        low_send[...] = mine.astype(bf16)
        for d in range(1, 4):
            c = remote(low_send, low_y.at[d - 1], sy_send.at[d - 1], sy_recv.at[d - 1], y_to[d - 1])
            c.start()
            sent.append(c)

    def send_low_back():
        total = low_part[core]
        for d in range(1, 4):
            sent[3 + d].wait_recv()
            total = total + low_y[d - 1].astype(f32)
        low[core] = total.astype(bf16)
        c = remote(low.at[core], low.at[core], sc_send.at[1], sc_recv.at[1], other)
        c.start()
        sent.append(c)

    steps = {STEP_CORE: send_low_core, STEP_Y: send_low_y, STEP_BACK: send_low_back}
    units = [(h, i) for h in range(HEADS) for i in range(BLOCKS)]
    held = None
    for n, (h, i) in enumerate(units):
        ready = scores(h, i)
        if held is not None:
            mix(*held)
        held = (h, i, *ready)
        if n in steps:
            steps[n]()
    mix(*held)

    sent[7].wait_recv()
    grad = dot(low[0], mixed[:HALF, :]) + dot(low[1], mixed[HALF:, :])
    grads[0] = (grad * LEN ** (-0.5)).astype(bf16)
    sent_z = []
    for d in range(7, 0, -1):
        c = remote(grads.at[0], grads.at[d], sz_send.at[d - 1], sz_recv.at[d - 1], z_to[d - 1])
        c.start()
        sent_z.append(c)
    for c in sent[1:4]:
        c.wait_recv()
    columns = jnp.concatenate([vec[d] for d in range(4)], axis=1)
    for c in sent_z:
        c.wait_recv()

    ordered = dot(perm[...], grads[...].reshape(8 * RANK, COLS)).astype(bf16)
    part[...] = dot(ordered, columns).reshape(2, 64, 512)
    c = remote(part.at[1 - core], part_core, sc_send.at[2], sc_recv.at[2], other)
    c.start()
    c.wait_recv()
    sent.append(c)
    part[core] = part[core] + part_core[...]
    rot_send[...] = part[core].reshape(4, 16, 512).astype(bf16)
    sent_y = []
    for d in range(1, 4):
        c = remote(
            rot_send.at[lax.rem(y + d, 4)], rot_y.at[d - 1], sy_send.at[2 + d], sy_recv.at[2 + d], y_to[d - 1]
        )
        c.start()
        sent_y.append(c)
    rotated = part[core, pl.ds(pl.multiple_of(16 * y, 16), 16), :]
    for d, c in enumerate(sent_y):
        c.wait_recv()
        rotated = rotated + rot_y[d].astype(f32)
    squares = rotated * rotated
    pairs = squares[:8] + squares[8:]
    pairs = pairs + pltpu.roll(pairs, 4, 0)
    pairs = pairs + pltpu.roll(pairs, 2, 0)
    for d in range(4):
        spec_send[d] = pairs[:, 128 * d : 128 * (d + 1)]
    sent_x = []
    for d in range(1, 4):
        c = remote(spec_send.at[d], spec_x.at[d - 1], sx_send.at[2 + d], sx_recv.at[2 + d], x_from[d - 1])
        c.start()
        sent_x.append(c)
    total = spec_send[0]
    for d, c in enumerate(sent_x):
        c.wait_recv()
        total = total + spec_x[d]
    out_ref[...] = total[:2]
    for c in sent + sent_z + sent_y + sent_x:
        c.wait_send()


STEP_CORE, STEP_Y, STEP_BACK = 19, 22, 30


def shards(queries, keys, values, documents, cotangent, up, vectors):
    vmem = pltpu.VMEM
    dma = pltpu.SemaphoreType.DMA
    summed = pl.pallas_call(
        kernel,
        out_shape=jax.ShapeDtypeStruct((2, 128), f32),
        in_specs=[pl.BlockSpec(memory_space=pl.ANY)] * 7,
        out_specs=pl.BlockSpec(memory_space=pltpu.VMEM),
        scratch_shapes=[
            vmem((LEN, COLS), bf16),
            vmem((LEN, COLS), bf16),
            vmem((LEN, COLS), bf16),
            vmem((1, LEN), jnp.int32),
            vmem((LEN, FEATURES), bf16),
            vmem((FEATURES, RANK), bf16),
            vmem((4, COLS, 128), bf16),
            vmem((LEN, HEAD_DIM), bf16),
            vmem((LEN, HEAD_DIM), bf16),
            vmem((128, 128), bf16),
            vmem((LEN, COLS), bf16),
            vmem((2, RANK, HALF), f32),
            vmem((RANK, HALF), f32),
            vmem((RANK, HALF), bf16),
            vmem((3, RANK, HALF), bf16),
            vmem((2, RANK, HALF), bf16),
            vmem((8, RANK, COLS), bf16),
            vmem((2, 64, 512), f32),
            vmem((64, 512), f32),
            vmem((4, 16, 512), bf16),
            vmem((3, 16, 512), bf16),
            vmem((4, 8, 128), f32),
            vmem((3, 8, 128), f32),
            dma((6,)),
            dma((4,)),
            dma((3,)),
            dma((3,)),
            dma((6,)),
            dma((6,)),
            dma((6,)),
            dma((6,)),
            dma((7,)),
            dma((7,)),
        ],
        compiler_params=pltpu.CompilerParams(
            collective_id=0, has_side_effects=True, vmem_limit_bytes=56 * 2**20
        ),
    )(queries, keys, values, documents, cotangent, up, vectors)
    return summed * (1.0 / SEQS)


def solution(mesh):
    return jax.shard_map(
        shards,
        mesh=mesh,
        in_specs=(
            P("dp", None, ("eig", "tensor")),
            P("dp", None, ("eig", "tensor")),
            P("dp", None, ("eig", "tensor")),
            P("dp", None),
            P("dp", None, ("eig", "tensor")),
            P(("eig", "tensor"), None),
            P(("eig", "tensor"), "dp"),
        ),
        out_specs=P(("eig", "tensor"), "dp"),
        check_vma=False,
    )
```

time: 445 us -> 40.9 us (0.09)
  waiting for transfers between devices: 279 us -> 0 us
  matrix products: 90.5 us -> 0 us
  Pallas kernels: 0 us -> 37.9 us
  blocking collectives: 27.7 us -> 0 us
  local copies, waits for them, and re-layouts: 20.7 us -> 1.59 us
  between operations: 13.8 us -> 0.01 us
  other arithmetic: 6.28 us -> 1.23 us
    unnamed x5 -> x0, waiting for transfers between devices: 279 us -> none
    sub x4 -> x0, matrix products: 45.6 us -> none  [attend_block(): expon = jnp.exp(scores - row_max)]
    dot_general x6 -> x0, matrix products: 44.9 us -> none  [the longest x4 37.6 us: attend_block(): jnp.einsum('hqk,khd->qhd', weights, split_v, preferred_element_type=jnp.f...]
    pallas_call x0 -> x1, Pallas kernels: none -> 37.9 us  [shards(): pl.pallas_call(kernel, out_shape=jax.ShapeDtypeStruct((2, 128), f32), in_...]
    psum x1 -> x0, blocking collectives: 27.7 us -> none  [shards(): lax.psum(lower_portion, ('eig', 'tensor')).astype(jnp.bfloat16)]
    unnamed x15 -> x1, local copies, waits for them, and re-layouts: 17 us -> 1.59 us
    and x4 -> x0, other arithmetic: 4.76 us -> none  [attend_block(): (query_doc[:, None] == document[None, :]) & (position[None, :] <= query_p...]
  transfers between devices with their start and end apart: 3 -> 0, of which waited for: 2 -> 0; matrix products, arithmetic and copies ran while one was open for 25% -> 0% of each run, Pallas kernels for 0% -> 0%
where the time goes in v1:
time: 40.9 us; the launch traced here: 40.7 us
  Pallas kernels  37.9 us (93%)
  local copies, waits for them, and re-layouts  1.59 us (4%)
  other arithmetic  1.23 us (3%)
    pallas_call x1, Pallas kernels, shards(): pl.pallas_call(kernel, out_shape=jax.ShapeDtypeStruct((2, 128), f32), in_...  37.9 us
    unnamed x1, local copies, waits for them, and re-layouts  1.59 us
    mul x1, other arithmetic, shards(): return summed * (1.0 / SEQS)  1.23 us

profile of v1, /device:TPU:1, one launch (start us, length us, event | category | flops | bytes accessed | tf_op | source)
XLA Modules:
  0.0 40.7 jit_solution(7731230192360385910)
XLA Ops:
  0.0 1.6 %copy.8.up_hbm = bf16[1024,16]{1,0:T(8,128)(2,1)} copy(bf16[1024,16]{0,1:T(8,128)(2,1)} %param.12) | data formatting | bytes 65536 | tf_op args[5]
  1.6 37.9 %shard_map.73 = f32[2,128]{1,0:T(2,128)} custom-call(bf16[1,2048,512]{2,1,0:T(8,128)(2,1)} %q_hbm.1, bf16[1,2048,512]{2,1,0:T(8,128)(2,1)} %k_hbm.1, bf16[1,2048,512]{2,1,0:T(8,128)(2,1)} %v_hbm.1, s32[1,2048]{1,0:T(1,128)} %doc_hbm.1, bf16[1,2048,1024]{2,1,0:T(8,128)(2,1)} %cot_hbm.1, bf16[1024,16]{1,0:T(8,128)(2,1)} %copy.8.up_hbm, bf16[512,128]{1,0:T(8,128)(2,1)} %vec_hbm.1), custom_call_target="tpu_custom_call" | custom-call | tf_op jit(solution)/shard_map/pallas_call | solution.py:253
  39.5 1.2 %broadcast_multiply_fusion = f32[2,128]{1,0:T(2,128)} fusion(f32[2,128]{1,0:T(2,128)} %shard_map.73), kind=kLoop, calls=%fused_computation | loop fusion | flops 256 | bytes 2048 | tf_op jit(solution)/shard_map/mul | solution.py:297

commit v2 on v1

--- a/solution.py
+++ b/solution.py
@@ -45,7 +45,7 @@
     q, k, v, doc, cot, up, vec, kx, qx, perm, mixed,
     low_part, low_core, low_send, low_y, low,
     grads, part, part_core, rot_send, rot_y, spec_send, spec_x,
-    in_sem, cot_sem, sc_send, sc_recv, sy_send, sy_recv, sx_send, sx_recv, sz_send, sz_recv,
+    in_sem, cot_sem, row_sem, sc_send, sc_recv, sy_send, sy_recv, sx_send, sx_recv, sz_send, sz_recv,
 ):
     z, x, y, core = places()
     other = device(z, x, y, 1 - core)
@@ -66,31 +66,23 @@
 
     loads = [
         pltpu.make_async_copy(src, dst, in_sem.at[n])
-        for n, (src, dst) in enumerate(
-            [
-                (up_hbm, up),
-                (doc_hbm, doc),
-                (q_hbm.at[0], q),
-                (k_hbm.at[0], k),
-                (v_hbm.at[0], v),
-                (vec_hbm, vec.at[0]),
-            ]
-        )
+        for n, (src, dst) in enumerate([(doc_hbm, doc), (vec_hbm, vec.at[0]), (up_hbm, up)])
     ]
+    row_loads = []
+    for n in range(2):
+        at = pl.ds(512 if n else 0, 1536 if n else 512)
+        for m, (src, dst) in enumerate([(k_hbm, k), (q_hbm, q), (v_hbm, v)]):
+            row_loads.append(pltpu.make_async_copy(src.at[0, at, :], dst.at[at, :], row_sem.at[3 * n + m]))
     chunks = [
         pltpu.make_async_copy(
             cot_hbm.at[0, pl.ds(512 * c, 512), :], cot.at[pl.ds(512 * c, 512), :], cot_sem.at[c]
         )
         for c in range(4)
     ]
-    loads[0].start()
-    loads[1].start()
-    for c in chunks:
-        c.start()
-    for c in loads[2:]:
-        c.start()
-
-    loads[1].wait()
+    for c in loads + row_loads[:3]:
+        c.start()
+
+    loads[0].wait()
     one_hot = jnp.where(
         lax.broadcasted_iota(jnp.int32, (HEAD_DIM, LEN), 0) == doc[...], 1.0, 0.0
     ).astype(f32)
@@ -102,16 +94,6 @@
         16 * ((row >> 1) & 7) + 8 * ((row >> 4) & 1) + 4 * ((row >> 5) & 1) + 2 * (row >> 6) + (row & 1)
     )
     perm[...] = jnp.where(lax.broadcasted_iota(jnp.int32, (128, 128), 1) == source, 1.0, 0.0).astype(bf16)
-
-    loads[0].wait()
-    up_t = up[...].astype(f32).T.astype(bf16)
-    for c in range(4):
-        chunks[c].wait()
-        low_part[c // 2, :, pl.ds(512 * (c % 2), 512)] = dot(
-            up_t, cot[512 * c : 512 * (c + 1), :], 1, 1
-        )
-    for c in loads[2:]:
-        c.wait()
 
     lower = lax.broadcasted_iota(jnp.int32, (BLOCK, BLOCK), 1) <= lax.broadcasted_iota(
         jnp.int32, (BLOCK, BLOCK), 0
@@ -149,15 +131,25 @@
 
     sent = []
 
+    def project():
+        loads[2].wait()
+        for c in range(4):
+            chunks[c].wait()
+            if c == 1:
+                for load in row_loads[3:]:
+                    load.start()
+            low_part[c // 2, :, pl.ds(512 * (c % 2), 512)] = dot(
+                up[...], cot[512 * c : 512 * (c + 1), :], 1, 1
+            )
+        loads[1].wait()
+        for c in row_loads[3:]:
+            c.wait()
+
     def send_low_core():
         pl.semaphore_wait(barrier, len(peers))
         c = remote(low_part.at[1 - core], low_core, sc_send.at[0], sc_recv.at[0], other)
         c.start()
         sent.append(c)
-        for d in range(1, 4):
-            e = remote(vec.at[0], vec.at[d], sx_send.at[d - 1], sx_recv.at[d - 1], x_to[d - 1])
-            e.start()
-            sent.append(e)
 
     def send_low_y():
         sent[0].wait_recv()
@@ -168,38 +160,65 @@
             c = remote(low_send, low_y.at[d - 1], sy_send.at[d - 1], sy_recv.at[d - 1], y_to[d - 1])
             c.start()
             sent.append(c)
+        for d in range(1, 4):
+            c = remote(vec.at[0], vec.at[d], sx_send.at[d - 1], sx_recv.at[d - 1], x_to[d - 1])
+            c.start()
+            sent.append(c)
 
     def send_low_back():
         total = low_part[core]
         for d in range(1, 4):
-            sent[3 + d].wait_recv()
+            sent[d].wait_recv()
             total = total + low_y[d - 1].astype(f32)
         low[core] = total.astype(bf16)
         c = remote(low.at[core], low.at[core], sc_send.at[1], sc_recv.at[1], other)
         c.start()
         sent.append(c)
 
-    steps = {STEP_CORE: send_low_core, STEP_Y: send_low_y, STEP_BACK: send_low_back}
-    units = [(h, i) for h in range(HEADS) for i in range(BLOCKS)]
+    def early_gradient():
+        sent[7].wait_recv()
+        send_gradient(0)
+
+    sent_z = []
+
+    def send_gradient(n):
+        hs = slice(0, 384) if n == 0 else slice(384, 512)
+        grad = dot(low[0], mixed[:HALF, hs]) + dot(low[1], mixed[HALF:, hs])
+        grads[0, :, hs] = (grad * LEN ** (-0.5)).astype(bf16)
+        for d in range(7, 0, -1):
+            at = 7 * n + d - 1
+            c = remote(
+                grads.at[0, :, pl.ds(384 * n, 128 if n else 384)],
+                grads.at[d, :, pl.ds(384 * n, 128 if n else 384)],
+                sz_send.at[at],
+                sz_recv.at[at],
+                z_to[d - 1],
+            )
+            c.start()
+            sent_z.append(c)
+
+    units = [(h, i) for h in range(HEADS) for i in range(2)]
+    units += [(h, i) for h in range(HEADS) for i in range(2, BLOCKS)]
+    events = [(12, project), (PLAN[0], send_low_core), (PLAN[1], send_low_y), (PLAN[2], send_low_back)]
+    events.append((PLAN[3], early_gradient))
+    done = 0
+    for c in row_loads[:3]:
+        c.wait()
+    for c in chunks:
+        c.start()
     held = None
-    for n, (h, i) in enumerate(units):
+    for h, i in units:
         ready = scores(h, i)
         if held is not None:
             mix(*held)
         held = (h, i, *ready)
-        if n in steps:
-            steps[n]()
+        done += len(ready[1])
+        while events and events[0][0] <= done:
+            events.pop(0)[1]()
     mix(*held)
 
-    sent[7].wait_recv()
-    grad = dot(low[0], mixed[:HALF, :]) + dot(low[1], mixed[HALF:, :])
-    grads[0] = (grad * LEN ** (-0.5)).astype(bf16)
-    sent_z = []
-    for d in range(7, 0, -1):
-        c = remote(grads.at[0], grads.at[d], sz_send.at[d - 1], sz_recv.at[d - 1], z_to[d - 1])
-        c.start()
-        sent_z.append(c)
-    for c in sent[1:4]:
+    send_gradient(1)
+    for c in sent[4:7]:
         c.wait_recv()
     columns = jnp.concatenate([vec[d] for d in range(4)], axis=1)
     for c in sent_z:
@@ -244,7 +263,7 @@
         c.wait_send()
 
 
-STEP_CORE, STEP_Y, STEP_BACK = 19, 22, 30
+PLAN = (20, 34, 92, 108)
 
 
 def shards(queries, keys, values, documents, cotangent, up, vectors):
@@ -261,7 +280,7 @@
             vmem((LEN, COLS), bf16),
             vmem((1, LEN), jnp.int32),
             vmem((LEN, FEATURES), bf16),
-            vmem((FEATURES, RANK), bf16),
+            vmem((RANK, FEATURES), bf16),
             vmem((4, COLS, 128), bf16),
             vmem((LEN, HEAD_DIM), bf16),
             vmem((LEN, HEAD_DIM), bf16),
@@ -279,21 +298,22 @@
             vmem((3, 16, 512), bf16),
             vmem((4, 8, 128), f32),
             vmem((3, 8, 128), f32),
-            dma((6,)),
+            dma((3,)),
             dma((4,)),
+            dma((6,)),
             dma((3,)),
             dma((3,)),
             dma((6,)),
             dma((6,)),
             dma((6,)),
             dma((6,)),
-            dma((7,)),
-            dma((7,)),
+            dma((14,)),
+            dma((14,)),
         ],
         compiler_params=pltpu.CompilerParams(
             collective_id=0, has_side_effects=True, vmem_limit_bytes=56 * 2**20
         ),
-    )(queries, keys, values, documents, cotangent, up, vectors)
+    )(queries, keys, values, documents, cotangent, up.T, vectors)
     return summed * (1.0 / SEQS)
 
 

time: 40.9 us -> 38.8 us (0.949)
  local copies, waits for them, and re-layouts: 1.59 us -> 0 us
  Pallas kernels: 37.9 us -> 37.4 us
    unnamed x1 -> x0, local copies, waits for them, and re-layouts: 1.59 us -> none
    pallas_call x1, Pallas kernels: 37.9 us -> 37.4 us  [shards(): pl.pallas_call(kernel, out_shape=jax.ShapeDtypeStruct((2, 128), f32), in_...]
where the time goes in v2:
time: 38.8 us; the launch traced here: 38.6 us
  Pallas kernels  37.4 us (96%)
  other arithmetic  1.24 us (3%)
    pallas_call x1, Pallas kernels, shards(): pl.pallas_call(kernel, out_shape=jax.ShapeDtypeStruct((2, 128), f32), in_...  37.4 us
    mul x1, other arithmetic, shards(): return summed * (1.0 / SEQS)  1.24 us

profile of v2, /device:TPU:1, one launch (start us, length us, event | category | flops | bytes accessed | tf_op | source)
XLA Modules:
  0.0 38.6 jit_solution(13455154070018165209)
XLA Ops:
  0.0 37.4 %shard_map.73 = f32[2,128]{1,0:T(2,128)} custom-call(bf16[1,2048,512]{2,1,0:T(8,128)(2,1)} %q_hbm.1, bf16[1,2048,512]{2,1,0:T(8,128)(2,1)} %k_hbm.1, bf16[1,2048,512]{2,1,0:T(8,128)(2,1)} %v_hbm.1, s32[1,2048]{1,0:T(1,128)} %doc_hbm.1, bf16[1,2048,1024]{2,1,0:T(8,128)(2,1)} %cot_hbm.1, bf16[16,1024]{1,0:T(8,128)(2,1)} %bitcast.1, bf16[512,128]{1,0:T(8,128)(2,1)} %vec_hbm.1), custom_call_target="tpu_custom_call" | custom-call | tf_op jit(solution)/shard_map/pallas_call | solution.py:272
  37.4 1.2 %broadcast_multiply_fusion = f32[2,128]{1,0:T(2,128)} fusion(f32[2,128]{1,0:T(2,128)} %shard_map.73), kind=kLoop, calls=%fused_computation | loop fusion | flops 256 | bytes 2048 | tf_op jit(solution)/shard_map/mul | solution.py:317

commit v3 on v2

--- a/solution.py
+++ b/solution.py
@@ -42,7 +42,7 @@
 
 def kernel(
     q_hbm, k_hbm, v_hbm, doc_hbm, cot_hbm, up_hbm, vec_hbm, out_ref,
-    q, k, v, doc, cot, up, vec, kx, qx, perm, mixed,
+    q, k, v, doc, cot, up, vec, kx, qx, whole, mixed,
     low_part, low_core, low_send, low_y, low,
     grads, part, part_core, rot_send, rot_y, spec_send, spec_x,
     in_sem, cot_sem, row_sem, sc_send, sc_recv, sy_send, sy_recv, sx_send, sx_recv, sz_send, sz_recv,
@@ -59,10 +59,6 @@
         return pltpu.make_async_remote_copy(
             src_ref=src, dst_ref=dst, send_sem=send, recv_sem=recv, device_id=to, device_id_type=MESH
         )
-
-    barrier = pltpu.get_barrier_semaphore()
-    for peer in peers:
-        pl.semaphore_signal(barrier, inc=1, device_id=peer, device_id_type=MESH)
 
     loads = [
         pltpu.make_async_copy(src, dst, in_sem.at[n])
@@ -79,8 +75,11 @@
         )
         for c in range(4)
     ]
-    for c in loads + row_loads[:3]:
-        c.start()
+    for c in row_loads[:3] + loads + chunks[:1]:
+        c.start()
+    barrier = pltpu.get_barrier_semaphore()
+    for peer in peers:
+        pl.semaphore_signal(barrier, inc=1, device_id=peer, device_id_type=MESH)
 
     loads[0].wait()
     one_hot = jnp.where(
@@ -89,12 +88,6 @@
     turned = one_hot.T
     kx[...] = turned.astype(bf16)
     qx[...] = jnp.where(turned > 0.5, 0.0, NEG).astype(bf16)
-    row = lax.broadcasted_iota(jnp.int32, (128, 128), 0)
-    source = (
-        16 * ((row >> 1) & 7) + 8 * ((row >> 4) & 1) + 4 * ((row >> 5) & 1) + 2 * (row >> 6) + (row & 1)
-    )
-    perm[...] = jnp.where(lax.broadcasted_iota(jnp.int32, (128, 128), 1) == source, 1.0, 0.0).astype(bf16)
-
     lower = lax.broadcasted_iota(jnp.int32, (BLOCK, BLOCK), 1) <= lax.broadcasted_iota(
         jnp.int32, (BLOCK, BLOCK), 0
     )
@@ -135,7 +128,7 @@
         loads[2].wait()
         for c in range(4):
             chunks[c].wait()
-            if c == 1:
+            if c == 0:
                 for load in row_loads[3:]:
                     load.start()
             low_part[c // 2, :, pl.ds(512 * (c % 2), 512)] = dot(
@@ -204,7 +197,7 @@
     done = 0
     for c in row_loads[:3]:
         c.wait()
-    for c in chunks:
+    for c in chunks[1:]:
         c.start()
     held = None
     for h, i in units:
@@ -224,8 +217,16 @@
     for c in sent_z:
         c.wait_recv()
 
-    ordered = dot(perm[...], grads[...].reshape(8 * RANK, COLS)).astype(bf16)
-    part[...] = dot(ordered, columns).reshape(2, 64, 512)
+    product = dot(grads[...].reshape(8 * RANK, COLS), columns)
+    for n in range(4):
+        whole[n] = product[:, 128 * n : 128 * (n + 1)]
+    for half in range(2):
+        for pair in range(8):
+            rank = 8 * (pair // 2 % 2) + 4 * (pair // 4) + 2 * half + pair % 2
+            for n in range(4):
+                part[half, 8 * pair : 8 * pair + 8, 128 * n : 128 * (n + 1)] = whole[
+                    n, pl.ds(rank, 8, stride=16), :
+                ]
     c = remote(part.at[1 - core], part_core, sc_send.at[2], sc_recv.at[2], other)
     c.start()
     c.wait_recv()
@@ -244,9 +245,12 @@
         c.wait_recv()
         rotated = rotated + rot_y[d].astype(f32)
     squares = rotated * rotated
-    pairs = squares[:8] + squares[8:]
-    pairs = pairs + pltpu.roll(pairs, 4, 0)
-    pairs = pairs + pltpu.roll(pairs, 2, 0)
+    sums = []
+    for half in (squares[:8], squares[8:]):
+        for n in (4, 2, 1):
+            half = half + pltpu.roll(half, n, 0)
+        sums.append(half)
+    pairs = jnp.where(lax.broadcasted_iota(jnp.int32, (8, COLS), 0) == 0, sums[0], sums[1])
     for d in range(4):
         spec_send[d] = pairs[:, 128 * d : 128 * (d + 1)]
     sent_x = []
@@ -258,12 +262,12 @@
     for d, c in enumerate(sent_x):
         c.wait_recv()
         total = total + spec_x[d]
-    out_ref[...] = total[:2]
+    out_ref[...] = total[:2] * (1.0 / SEQS)
     for c in sent + sent_z + sent_y + sent_x:
         c.wait_send()
 
 
-PLAN = (20, 34, 92, 108)
+PLAN = (14, 30, 92, 110)
 
 
 def shards(queries, keys, values, documents, cotangent, up, vectors):
@@ -284,7 +288,7 @@
             vmem((4, COLS, 128), bf16),
             vmem((LEN, HEAD_DIM), bf16),
             vmem((LEN, HEAD_DIM), bf16),
-            vmem((128, 128), bf16),
+            vmem((4, 128, 128), f32),
             vmem((LEN, COLS), bf16),
             vmem((2, RANK, HALF), f32),
             vmem((RANK, HALF), f32),
@@ -314,7 +318,7 @@
             collective_id=0, has_side_effects=True, vmem_limit_bytes=56 * 2**20
         ),
     )(queries, keys, values, documents, cotangent, up.T, vectors)
-    return summed * (1.0 / SEQS)
+    return summed
 
 
 def solution(mesh):

time: 38.8 us -> 38 us (0.979)
  other arithmetic: 1.24 us -> 0 us
  local copies, waits for them, and re-layouts: 0 us -> 1.24 us
  Pallas kernels: 37.4 us -> 36.6 us
    mul x1 -> x0, other arithmetic: 1.24 us -> none  [shards(): return summed * (1.0 / SEQS)]
    unnamed x0 -> x1, local copies, waits for them, and re-layouts: none -> 1.24 us
    pallas_call x1, Pallas kernels: 37.4 us -> 36.6 us  [shards(): pl.pallas_call(kernel, out_shape=jax.ShapeDtypeStruct((2, 128), f32), in_...]
where the time goes in v3:
time: 38 us; the launch traced here: 37.9 us
  Pallas kernels  36.6 us (96%)
  local copies, waits for them, and re-layouts  1.24 us (3%)
    pallas_call x1, Pallas kernels, shards(): pl.pallas_call(kernel, out_shape=jax.ShapeDtypeStruct((2, 128), f32), in_...  36.6 us
    unnamed x1, local copies, waits for them, and re-layouts  1.24 us

profile of v3, /device:TPU:1, one launch (start us, length us, event | category | flops | bytes accessed | tf_op | source)
XLA Modules:
  0.0 37.9 jit_solution(6193378510536450578)
XLA Ops:
  0.0 36.6 %shard_map.73 = f32[2,128]{1,0:T(2,128)} custom-call(bf16[1,2048,512]{2,1,0:T(8,128)(2,1)} %q_hbm.1, bf16[1,2048,512]{2,1,0:T(8,128)(2,1)} %k_hbm.1, bf16[1,2048,512]{2,1,0:T(8,128)(2,1)} %v_hbm.1, s32[1,2048]{1,0:T(1,128)} %doc_hbm.1, bf16[1,2048,1024]{2,1,0:T(8,128)(2,1)} %cot_hbm.1, bf16[16,1024]{1,0:T(8,128)(2,1)} %bitcast.1, bf16[512,128]{1,0:T(8,128)(2,1)} %vec_hbm.1), custom_call_target="tpu_custom_call" | custom-call | tf_op jit(solution)/shard_map/pallas_call | solution.py:276
  36.7 1.2 %copy.9 = f32[2,128]{1,0:T(2,128)} copy(f32[2,128]{1,0:T(2,128)} %shard_map.73) | data formatting | bytes 2048

commit v4 on v3

--- a/solution.py
+++ b/solution.py
@@ -178,7 +178,7 @@
         hs = slice(0, 384) if n == 0 else slice(384, 512)
         grad = dot(low[0], mixed[:HALF, hs]) + dot(low[1], mixed[HALF:, hs])
         grads[0, :, hs] = (grad * LEN ** (-0.5)).astype(bf16)
-        for d in range(7, 0, -1):
+        for d in (4, 3, 5, 2, 6, 1, 7):
             at = 7 * n + d - 1
             c = remote(
                 grads.at[0, :, pl.ds(384 * n, 128 if n else 384)],
@@ -214,10 +214,13 @@
     for c in sent[4:7]:
         c.wait_recv()
     columns = jnp.concatenate([vec[d] for d in range(4)], axis=1)
-    for c in sent_z:
-        c.wait_recv()
-
-    product = dot(grads[...].reshape(8 * RANK, COLS), columns)
+    for c in sent_z[:7]:
+        c.wait_recv()
+    product = dot(grads[:, :, :384].reshape(8 * RANK, 384), columns[:384])
+    for c in sent_z[7:]:
+        c.wait_recv()
+
+    product = product + dot(grads[:, :, 384:].reshape(8 * RANK, 128), columns[384:])
     for n in range(4):
         whole[n] = product[:, 128 * n : 128 * (n + 1)]
     for half in range(2):

time: 38 us -> 38 us (level)
  no operation moved by 1% of the time
where the time goes in v4:
time: 38 us; the launch traced here: 37.9 us
  Pallas kernels  36.7 us (97%)
  local copies, waits for them, and re-layouts  1.24 us (3%)
    pallas_call x1, Pallas kernels, shards(): pl.pallas_call(kernel, out_shape=jax.ShapeDtypeStruct((2, 128), f32), in_...  36.7 us
    unnamed x1, local copies, waits for them, and re-layouts  1.24 us

profile of v4, /device:TPU:1, one launch (start us, length us, event | category | flops | bytes accessed | tf_op | source)
XLA Modules:
  0.0 37.9 jit_solution(17412793925416733613)
XLA Ops:
  0.0 36.7 %shard_map.73 = f32[2,128]{1,0:T(2,128)} custom-call(bf16[1,2048,512]{2,1,0:T(8,128)(2,1)} %q_hbm.1, bf16[1,2048,512]{2,1,0:T(8,128)(2,1)} %k_hbm.1, bf16[1,2048,512]{2,1,0:T(8,128)(2,1)} %v_hbm.1, s32[1,2048]{1,0:T(1,128)} %doc_hbm.1, bf16[1,2048,1024]{2,1,0:T(8,128)(2,1)} %cot_hbm.1, bf16[16,1024]{1,0:T(8,128)(2,1)} %bitcast.1, bf16[512,128]{1,0:T(8,128)(2,1)} %vec_hbm.1), custom_call_target="tpu_custom_call" | custom-call | tf_op jit(solution)/shard_map/pallas_call | solution.py:279
  36.7 1.2 %copy.9 = f32[2,128]{1,0:T(2,128)} copy(f32[2,128]{1,0:T(2,128)} %shard_map.73) | data formatting | bytes 2048
